TPU v7x, 32 devices: a whole 2x2x4 slice. The times are simulated.
32 devices in a mesh: section: 4 (over z), dp: 8 (over y, x, core).
Axes of the slice: x: 2, y: 2, z: 4, core: 2. Of those that a mesh axis runs over, the one named last changes fastest.
Arguments:
- section_inputs: bfloat16 [4, 2048, 896], P('section', 'dp'), may hold values from -44 to 44
- cotangent: bfloat16 [2048, 896], P('dp'), may hold values from -6 to 6
- norm_gain: float32 [4, 896], P('section'), may hold values from 0.25 to 1.75
- quant_gate: bfloat16 [4, 896, 2432], P('section', 'dp'), may hold values from -1 to 1
- quant_up: bfloat16 [4, 896, 2432], P('section', 'dp'), may hold values from -1 to 1
- scales: float32 [4, 2], P('section'), may hold values from 0.04 to 0.08
- down_proj: bfloat16 [4, 2432, 896], P('section'), may hold values from -0.125 to 0.125
- master_gate: float32 [4, 896, 2432], P('section', 'dp'), may hold values from -0.3 to 0.3
- master_up: float32 [4, 896, 2432], P('section', 'dp'), may hold values from -0.3 to 0.3
- moment_gate: float32 [4, 896, 2432], P('section', 'dp'), may hold values from -3 to 3
- moment_up: float32 [4, 896, 2432], P('section', 'dp'), may hold values from -3 to 3
- second_gate: float32 [4, 896, 2432], P('section', 'dp'), may hold values from 0.05 to 1
- second_up: float32 [4, 896, 2432], P('section', 'dp'), may hold values from 0.05 to 1
- next_inputs: bfloat16 [4, 2048, 896], P('section', 'dp'), may hold values from -44 to 44
Outputs:
- input_grads: bfloat16 [4, 2048, 896], P('section', 'dp')
- master_gate_new: float32 [4, 896, 2432], P('section', 'dp')
- master_up_new: float32 [4, 896, 2432], P('section', 'dp')
- moment_gate_new: float32 [4, 896, 2432], P('section', 'dp')
- moment_up_new: float32 [4, 896, 2432], P('section', 'dp')
- second_gate_new: float32 [4, 896, 2432], P('section', 'dp')
- second_up_new: float32 [4, 896, 2432], P('section', 'dp')
- new_scales: float32 [4, 2], P('section')
- next_hidden: bfloat16 [4, 2048, 2432], P('section', 'dp')
All inputs are finite; a program needn't handle non-finite values. Where the computation divides by a largest or mean magnitude, that divisor is 1e-20 or more.
Results may differ from a plain program's by a relative error of at most 0.034.
Values may be sent and summed in bfloat16 or wider, within the bound.
No kernel may reach another device: no remote copies, remote signals or barrier semaphores. Data moves between devices by JAX's collectives and lax.ppermute only.
A program may use at most 128 MiB of HBM per device.

v0:
```python
import jax
import jax.numpy as jnp
from jax import lax
from jax.sharding import PartitionSpec as P

beta_one = 0.9
beta_two = 0.95
learn_rate = 0.002
decay_rate = 0.1
adam_steps = 100.0
norm_eps = 1e-06
adam_eps = 1e-08
scale_eps = 1e-06


def shifted(value, axis, steps):
    count = lax.axis_size(axis)
    first, last = (max(0, -steps), min(count, count - steps))
    return lax.ppermute(value, axis, [(source, source + steps) for source in range(first, last)])


def normalize(inputs, norm_gain):
    widened = inputs.astype(jnp.float32)
    inverse = lax.rsqrt(jnp.mean(widened * widened, axis=-1, keepdims=True) + norm_eps)
    return (widened, inverse, (widened * inverse * norm_gain).astype(jnp.bfloat16))


def silu_slope(preact):
    sigmoid = jax.nn.sigmoid(preact)
    return (preact * sigmoid, sigmoid * (1.0 + preact * (1.0 - sigmoid)))


def transposed(first_op, second_op):
    return lax.dot_general(
        first_op, second_op, (((1,), (1,)), ((), ())), preferred_element_type=jnp.float32
    )


def block_back(
    widened, inverse, normed, norm_gain, gate_full, up_full, scale_pair, down_full, upstream
):
    gate_pre = jnp.dot(normed, gate_full, preferred_element_type=jnp.float32) * scale_pair[0]
    up_pre = jnp.dot(normed, up_full, preferred_element_type=jnp.float32) * scale_pair[1]
    hidden_grad = transposed(upstream, down_full)
    active, slopes = silu_slope(gate_pre)
    gate_grad = (hidden_grad * up_pre * slopes).astype(jnp.bfloat16)
    up_grad = (hidden_grad * active).astype(jnp.bfloat16)
    normed_grad = (
        transposed(gate_grad, gate_full) * scale_pair[0]
        + transposed(up_grad, up_full) * scale_pair[1]
    )
    gained = norm_gain * normed_grad
    mean_term = jnp.mean(widened * gained, axis=-1, keepdims=True)
    result = (
        upstream.astype(jnp.float32)
        + inverse * gained
        - widened * (inverse * inverse * inverse) * mean_term
    )
    return (result.astype(jnp.bfloat16), jnp.concatenate([gate_grad, up_grad], axis=1))


def adam_update(master, moment_old, second_old, gradient):
    moment_one = beta_one * moment_old + (1.0 - beta_one) * gradient
    moment_two = beta_two * second_old + (1.0 - beta_two) * gradient * gradient
    unbiased_one = moment_one / (1.0 - beta_one**adam_steps)
    unbiased_two = moment_two / (1.0 - beta_two**adam_steps)
    updated = master - learn_rate * (
        unbiased_one / (jnp.sqrt(unbiased_two) + adam_eps) + decay_rate * master
    )
    return (updated, moment_one, moment_two)


def shards(
    section_inputs,
    cotangent,
    norm_gain,
    quant_gate,
    quant_up,
    scales,
    down_proj,
    master_gate,
    master_up,
    moment_gate,
    moment_up,
    second_gate,
    second_up,
    next_inputs,
):
    gain_row = norm_gain[0]
    scale_pair = scales[0]
    down_local = down_proj[0]
    tok_rows = section_inputs.shape[1]
    feature_count = section_inputs.shape[2]
    hidden_count = quant_gate.shape[2]
    sections = lax.axis_size("section")
    position = lax.axis_index("section")
    gate_full, up_full = (
        lax.all_gather(quant_gate[0], "dp", axis=0, tiled=True),
        lax.all_gather(quant_up[0], "dp", axis=0, tiled=True),
    )
    widened, inverse, normed = normalize(section_inputs[0], gain_row)
    blocks = tok_rows // tok_rows
    turn_count = sections + blocks - 1
    last_section = sections - 1

    def one_turn(turn_index, loop_state):
        incoming, grads_all, result_all = loop_state
        micro_index = turn_index - (last_section - position)
        is_active = jnp.logical_and(micro_index >= 0, micro_index < blocks)
        upstream = jnp.where(position == last_section, cotangent, incoming)

        def working(buffers):
            result, grads_both = block_back(
                widened,
                inverse,
                normed,
                gain_row,
                gate_full,
                up_full,
                scale_pair,
                down_local,
                upstream,
            )
            return (result, (grads_both, result))

        def resting(buffers):
            return (jnp.zeros((tok_rows, feature_count), jnp.bfloat16), buffers)

        outgoing, stored = lax.cond(is_active, working, resting, (grads_all, result_all))
        incoming = shifted(outgoing, "section", -1)
        return (incoming, stored[0], stored[1])

    start_state = (
        jnp.zeros((tok_rows, feature_count), jnp.bfloat16),
        jnp.zeros((tok_rows, 2 * hidden_count), jnp.bfloat16),
        jnp.zeros((tok_rows, feature_count), jnp.bfloat16),
    )
    incoming, grads_all, result_all = lax.fori_loop(0, turn_count, one_turn, start_state)
    columns = normed
    summed = lax.psum_scatter(
        lax.dot_general(
            columns, grads_all, (((0,), (0,)), ((), ())), preferred_element_type=jnp.float32
        ).astype(jnp.bfloat16),
        "dp",
        scatter_dimension=0,
        tiled=True,
    ).astype(jnp.float32)
    new_gate, mom_gate, sec_gate = adam_update(
        master_gate[0], moment_gate[0], second_gate[0], summed[:, :hidden_count]
    )
    new_up, mom_up, sec_up = adam_update(
        master_up[0], moment_up[0], second_up[0], summed[:, hidden_count:]
    )
    peak_pair = lax.pmax((jnp.max(jnp.abs(new_gate)), jnp.max(jnp.abs(new_up))), "dp")
    scale_gate = peak_pair[0] + scale_eps
    scale_up = peak_pair[1] + scale_eps
    quant_next_gate = (new_gate / scale_gate).astype(jnp.bfloat16)
    quant_next_up = (new_up / scale_up).astype(jnp.bfloat16)
    unused_one, unused_two, next_normed = normalize(next_inputs[0], gain_row)
    stacked = jnp.concatenate([quant_next_gate, quant_next_up], axis=1)
    columns = next_normed
    gathered_sum = jnp.dot(
        columns,
        lax.all_gather(stacked, "dp", axis=0, tiled=True),
        preferred_element_type=jnp.float32,
    )
    gate_next = gathered_sum[:, :hidden_count] * scale_gate
    up_next = gathered_sum[:, hidden_count:] * scale_up
    next_hidden = (jax.nn.silu(gate_next) * up_next).astype(jnp.bfloat16)
    return (
        result_all[None],
        new_gate[None],
        new_up[None],
        mom_gate[None],
        mom_up[None],
        sec_gate[None],
        sec_up[None],
        jnp.stack([scale_gate, scale_up])[None, :],
        next_hidden[None],
    )


def solution(mesh):
    placed = (
        P("section", "dp", None),
        P("dp", None),
        P("section", None),
        P("section", "dp", None),
        P("section", "dp", None),
        P("section", None),
        P("section", None, None),
        P("section", "dp", None),
        P("section", "dp", None),
        P("section", "dp", None),
        P("section", "dp", None),
        P("section", "dp", None),
        P("section", "dp", None),
        P("section", "dp", None),
    )
    return jax.shard_map(
        shards,
        mesh=mesh,
        in_specs=placed,
        out_specs=(
            P("section", "dp", None),
            P("section", "dp", None),
            P("section", "dp", None),
            P("section", "dp", None),
            P("section", "dp", None),
            P("section", "dp", None),
            P("section", "dp", None),
            P("section", None),
            P("section", "dp", None),
        ),
        check_vma=False,
    )
```

profile of v0, /device:TPU:0, one launch (start us, length us, event | category | flops | bytes accessed | tf_op | source)
XLA Modules:
  0.0 414.8 jit_solution(5010772350669244574)
XLA Ops:
  9.4 1.2 multiply_reduce_fusion.1
  10.6 2.0 multiply_convert_fusion.1
  12.7 37.4 %all-gather.10.cloned.1.call-done = bf16[1,896,2432]{2,1,0:T(8,128)(2,1)} async-done(((bf16[1,112,2432]{2,1,0:T(8,128)(2,1)}), bf16[1,896,2432]{2,1,0:T(8,128)(2,1)}) %all-gather.10.cloned.1.call-update) | async-done | bytes 4358160 | tf_op jit(solution)/shard_map/all_gather | solution.py:98
  50.0 39.3 %all-gather.8.cloned.1.call-done = bf16[1,896,2432]{2,1,0:T(8,128)(2,1)} async-done(((bf16[1,112,2432]{2,1,0:T(8,128)(2,1)}), bf16[1,896,2432]{2,1,0:T(8,128)(2,1)}) %all-gather.8.cloned.1.call-update) | async-done | bytes 4358160 | tf_op jit(solution)/shard_map/all_gather | solution.py:99
  89.4 1.7 broadcast_in_dim.33
  91.9 151.1 %while.19 = (s32[]{:T(128)}, bf16[256,896]{1,0:T(8,128)(2,1)S(1)}, bf16[256,4864]{1,0:T(8,128)(2,1)}, bf16[256,896]{1,0:T(8,128)(2,1)}, s32[]{:T(128)}, /*index=...) while((s32[]{:T(128)}, bf16[256,896]{1,0:T(8,128)(2,1)S(1)}, ...), condition=%wide.region_5.6_spmd, body=%wide.region_1.5_spmd.sunk | while | flops 5598052864 | bytes 89869328 | solution.py:138
  92.7 1.3 collective-permute-start
  94.0 13.5 %collective-permute-done = bf16[256,896]{1,0:T(8,128)(2,1)S(1)} collective-permute-done((bf16[256,896]{1,0:T(8,128)(2,1)}, bf16[256,896]{1,0:T(8,128)(2,1)S(1)}, u32[]{:S(2)}, u32[]{:S(2)}) %collective-permute-start) | collective-permute-done | bytes 458784 | tf_op jit(solution)/shard_map/while/body/eval_jaxpr/ppermute | solution.py:19
  108.3 1.3 collective-permute-start
  109.6 12.7 %collective-permute-done = bf16[256,896]{1,0:T(8,128)(2,1)S(1)} collective-permute-done((bf16[256,896]{1,0:T(8,128)(2,1)}, bf16[256,896]{1,0:T(8,128)(2,1)S(1)}, u32[]{:S(2)}, u32[]{:S(2)}) %collective-permute-start) | collective-permute-done | bytes 458784 | tf_op jit(solution)/shard_map/while/body/eval_jaxpr/ppermute | solution.py:19
  123.0 1.3 collective-permute-start
  124.3 81.9 %collective-permute-done = bf16[256,896]{1,0:T(8,128)(2,1)S(1)} collective-permute-done((bf16[256,896]{1,0:T(8,128)(2,1)}, bf16[256,896]{1,0:T(8,128)(2,1)S(1)}, u32[]{:S(2)}, u32[]{:S(2)}) %collective-permute-start) | collective-permute-done | bytes 458784 | tf_op jit(solution)/shard_map/while/body/eval_jaxpr/ppermute | solution.py:19
  206.2 23.6 %conditional.2 = (bf16[256,896]{1,0:T(8,128)(2,1)}, bf16[256,4864]{1,0:T(8,128)(2,1)}, bf16[256,896]{1,0:T(8,128)(2,1)}) conditional(s32[]{:T(128)} %convert_element_type.81, (bf16[256,4864]{1,0:T(8,128)(2,1)}, bf16[256,896]{1,0:T(8,128)(2,1)}) %tuple.63, (pred[]{:T(512)}, bf16[256,896]{1,0:T(8,128)(2,1)}, bf16[256,896]{1,0:T(8,128)(2,1)S(1)}, ...), branch_computations={%region_2.2_spmd, %region_3.4_spmd} | conditional | flops 5598052864 | bytes 88033984 | solution.py:129
  206.9 5.1 %convolution_multiply_fusion = f32[256,2432]{1,0:T(8,128)S(1)} fusion(bf16[256,896]{1,0:T(8,128)(2,1)} %get-tuple-element.349, bf16[896,2432]{1,0:T(8,128)(2,1)} %get-tuple-element.352, f32[]{:T(128)} %bitcast.2), kind=kOutput, calls=%fused_computation | convolution fusion | flops 1116307456 | bytes 7307268 | tf_op jit(solution)/shard_map/while/body/eval_jaxpr/cond/branch_1_fun/dot_general | solution.py:42
  212.0 1.7 multiply_convert_fusion
  213.8 3.4 fusion.2
  217.2 3.1 convolution_multiply_fusion.2
  220.4 4.9 %multiply_reduce_fusion = (f32[256]{0:T(256)S(1)}, f32[256,896]{1,0:T(8,128)S(1)}) fusion(f32[256,896]{1,0:T(8,128)S(1)} %get-tuple-element.353, f32[256,896]{1,0:T(8,128)} %convolution_multiply_fusion.2, f32[]{:T(128)} %bitcast.2, bf16[256,2432]{1,0:T(8,128)(2,1)S(1)} %fusion.2, bf16[896,2432]{1,0:T(8,128)(2,1)} %get-tuple-element.352, f32[896]{0:T(1024)S(1)} %reduce), kind=kOutput, calls=%fused_computation.13 | convolution fusion | flops 1116831488 | bytes 8360452 | tf_op jit(solution)/shard_map/while/body/eval_jaxpr/cond/branch_1_fun/dot_general | solution.py:34
  225.3 1.1 subtract_convert_fusion
  226.4 1.8 copy.28
  228.2 1.7 pad_maximum_fusion
  229.9 1.3 collective-permute-start
  231.2 11.8 %collective-permute-done = bf16[256,896]{1,0:T(8,128)(2,1)S(1)} collective-permute-done((bf16[256,896]{1,0:T(8,128)(2,1)}, bf16[256,896]{1,0:T(8,128)(2,1)S(1)}, u32[]{:S(2)}, u32[]{:S(2)}) %collective-permute-start) | collective-permute-done | bytes 458784 | tf_op jit(solution)/shard_map/while/body/eval_jaxpr/ppermute | solution.py:19
  242.9 7.7 %convolution_convert_fusion = bf16[896,4864]{1,0:T(8,128)(2,1)} fusion(bf16[256,896]{1,0:T(8,128)(2,1)} %multiply_convert_fusion.1, bf16[256,4864]{1,0:T(8,128)(2,1)} %get-tuple-element.385), kind=kOutput, calls=%fused_computation.18 | convolution fusion | flops 2235727872 | bytes 11665408 | tf_op jit(solution)/shard_map/dot_general | solution.py:141
  250.9 70.1 %reduce-scatter.2.cloned.1.call-done = bf16[112,4864]{1,0:T(8,128)(2,1)} async-done(((bf16[896,4864]{1,0:T(8,128)(2,1)}), bf16[112,4864]{1,0:T(8,128)(2,1)}) %reduce-scatter.2.cloned.1.call-update) | async-done | bytes 1089552 | tf_op jit(solution)/shard_map/reduce_scatter | solution.py:140
  321.0 1.4 convert_element_type.58
  322.4 6.9 %abs_reduce_fusion.1 = (f32[]{:T(128)}, f32[112,2432]{1,0:T(8,128)S(1)}, f32[1,112,2432]{2,1,0:T(8,128)}, f32[1,112,2432]{2,1,0:T(8,128)}, f32[1,112,2432]{2,1,0...) fusion(f32[1,112,2432]{2,1,0:T(8,128)S(1)} %copy-done.6, ...), kind=kLoop, calls=%fused_computation.44 | loop fusion | flops 9261054 | bytes 15253512 | tf_op jit(solution)/shard_map/reduce_max | solution.py:154
  329.3 13.3 %all-reduce = (f32[]{:T(128)}, f32[]{:T(128)}) all-reduce(f32[]{:T(128)} %get-tuple-element.434, f32[]{:T(128)} %get-tuple-element.418), channel_id=1, replica_groups=mesh['section'=4,'dp'=8] {'dp'}, use_global_device_ids=true, to_apply=%region_10.11 | all-reduce | flops 2 | bytes 16 | tf_op jit(solution)/shard_map/pmax | solution.py:154
  344.1 1.1 pad_maximum_fusion.1
  345.9 55.1 %all-gather.6.cloned.1.call-done = bf16[896,4864]{1,0:T(8,128)(2,1)} async-done(((bf16[112,4864]{1,0:T(8,128)(2,1)}), bf16[896,4864]{1,0:T(8,128)(2,1)}) %all-gather.6.cloned.1.call-update) | async-done | bytes 8716304 | tf_op jit(solution)/shard_map/all_gather | solution.py:164
  401.0 5.5 %fusion.18 = f32[256,4864]{1,0:T(8,128)S(1)} fusion(bf16[896,4864]{1,0:T(8,128)(2,1)} %all-gather.6.cloned.1.call-done, bf16[1,256,896]{2,1,0:T(8,128)(2,1)S(1)} %copy-done.5, f32[256]{0:T(256)S(1)} %add_rsqrt_fusion, f32[896]{0:T(1024)S(1)} %reduce.1), kind=kOutput, calls=%fused_computation.50 | convolution fusion | flops 2232287232 | bytes 14160384 | tf_op jit(solution)/shard_map/dot_general | solution.py:162
  406.5 1.7 fusion.8
  (52 shorter events, 9.9 us)
Async XLA Ops:
  7.2 5.4 %copy-start.4 = (bf16[1,256,896]{2,1,0:T(8,128)(2,1)S(1)}, bf16[1,256,896]{2,1,0:T(8,128)(2,1)}, u32[]{:S(2)}) copy-start(bf16[1,256,896]{2,1,0:T(8,128)(2,1)} %param.18) | copy-start | bytes 1376260
  7.2 42.9 %all-gather.10.cloned.1.call-start = ((), (), s32[]{:S(2)}) async-start(), calls=%async_computation.4 | async-start | bytes 4902912 | tf_op jit(solution)/shard_map/all_gather | solution.py:98
  7.9 81.4 %all-gather.8.cloned.1.call-start = ((), (), s32[]{:S(2)}) async-start(), calls=%async_computation.3 | async-start | bytes 4902912 | tf_op jit(solution)/shard_map/all_gather | solution.py:99
  8.7 312.4 %reduce-scatter.2.cloned.1.call-start = ((), (), s32[]{:S(2)}) async-start(), calls=%async_computation.1 | async-start | bytes 9805824 | tf_op jit(solution)/shard_map/reduce_scatter | solution.py:140
  12.6 79.3 %copy-start.7 = (f32[1,896]{1,0:T(1,128)S(1)}, f32[1,896]{1,0:T(1,128)}, u32[]{:S(2)}) copy-start(f32[1,896]{1,0:T(1,128)} %param.20) | copy-start | bytes 10756
  12.6 79.3 %copy-start.8 = (f32[1,2]{1,0:T(1,128)S(1)}, f32[1,2]{1,0:T(1,128)}, u32[]{:S(2)}) copy-start(f32[1,2]{1,0:T(1,128)} %param.23) | copy-start | bytes 28
  92.7 14.8 %collective-permute-start = (bf16[256,896]{1,0:T(8,128)(2,1)}, bf16[256,896]{1,0:T(8,128)(2,1)S(1)}, u32[]{:S(2)}, u32[]{:S(2)}) collective-permute-start(bf16[256,896]{1,0:T(8,128)(2,1)} %get-tuple-element.532), channel_id=1, source_target_pairs={{8,0},{16,8},{24,16},{9,1},{17,9},{25,17},{10,2},{18,10},{26,18},{... | collective-permute-start | bytes 1376264 | tf_op jit(solution)/shard_map/while/body/eval_jaxpr/ppermute | solution.py:19
  108.3 14.0 %collective-permute-start = (bf16[256,896]{1,0:T(8,128)(2,1)}, bf16[256,896]{1,0:T(8,128)(2,1)S(1)}, u32[]{:S(2)}, u32[]{:S(2)}) collective-permute-start(bf16[256,896]{1,0:T(8,128)(2,1)} %get-tuple-element.532), channel_id=1, source_target_pairs={{8,0},{16,8},{24,16},{9,1},{17,9},{25,17},{10,2},{18,10},{26,18},{... | collective-permute-start | bytes 1376264 | tf_op jit(solution)/shard_map/while/body/eval_jaxpr/ppermute | solution.py:19
  123.0 83.2 %collective-permute-start = (bf16[256,896]{1,0:T(8,128)(2,1)}, bf16[256,896]{1,0:T(8,128)(2,1)S(1)}, u32[]{:S(2)}, u32[]{:S(2)}) collective-permute-start(bf16[256,896]{1,0:T(8,128)(2,1)} %get-tuple-element.532), channel_id=1, source_target_pairs={{8,0},{16,8},{24,16},{9,1},{17,9},{25,17},{10,2},{18,10},{26,18},{... | collective-permute-start | bytes 1376264 | tf_op jit(solution)/shard_map/while/body/eval_jaxpr/ppermute | solution.py:19
  206.2 5.8 %copy-start = (bf16[256,896]{1,0:T(8,128)(2,1)}, bf16[256,896]{1,0:T(8,128)(2,1)S(1)}, u32[]{:S(2)}) copy-start(bf16[256,896]{1,0:T(8,128)(2,1)S(1)} %get-tuple-element.345) | copy-start | bytes 1376260 | tf_op jit(solution)/shard_map/while/body/eval_jaxpr/cond
  206.9 5.1 %copy-start.9 = (bf16[2432,896]{1,0:T(8,128)(2,1)S(1)}, bf16[2432,896]{1,0:T(8,128)(2,1)}, u32[]{:S(2)}) copy-start(bf16[2432,896]{1,0:T(8,128)(2,1)} %get-tuple-element.348) | copy-start | bytes 13074436 | tf_op jit(solution)/shard_map/while/body/eval_jaxpr/cond
  206.9 6.9 %slice-start = ((s8[4358144]{0:T(1024)(128)(4,1)}), s8[4194304]{0:T(1024)(128)(4,1)S(1)}, s32[]{:S(2)}) async-start(s8[4358144]{0:T(1024)(128)(4,1)} %bitcast.107), calls=%async_computation.5 | async-start | bytes 8388608 | tf_op jit(solution)/shard_map/while/body/eval_jaxpr/cond
  212.0 1.8 slice-start.1
  220.4 4.9 %copy-start.1 = (bf16[256,896]{1,0:T(8,128)(2,1)S(1)}, bf16[256,896]{1,0:T(8,128)(2,1)}, u32[]{:S(2)}) copy-start(bf16[256,896]{1,0:T(8,128)(2,1)} %copy-done) | copy-start | bytes 1376260 | tf_op jit(solution)/shard_map/while/body/eval_jaxpr/cond
  229.9 13.1 %collective-permute-start = (bf16[256,896]{1,0:T(8,128)(2,1)}, bf16[256,896]{1,0:T(8,128)(2,1)S(1)}, u32[]{:S(2)}, u32[]{:S(2)}) collective-permute-start(bf16[256,896]{1,0:T(8,128)(2,1)} %get-tuple-element.532), channel_id=1, source_target_pairs={{8,0},{16,8},{24,16},{9,1},{17,9},{25,17},{10,2},{18,10},{26,18},{... | collective-permute-start | bytes 1376264 | tf_op jit(solution)/shard_map/while/body/eval_jaxpr/ppermute | solution.py:19
  250.7 71.7 %copy-start.6 = (f32[1,112,2432]{2,1,0:T(8,128)S(1)}, f32[1,112,2432]{2,1,0:T(8,128)}, u32[]{:S(2)}) copy-start(f32[1,112,2432]{2,1,0:T(8,128)} %param.29) | copy-start | bytes 3268612
  250.7 150.3 %all-gather.6.cloned.1.call-start = ((), (), s32[]{:S(2)}) async-start(), calls=%async_computation.2 | async-start | bytes 9805824 | tf_op jit(solution)/shard_map/all_gather | solution.py:164
  329.3 15.8 %copy-start.2 = (f32[112,2432]{1,0:T(8,128)}, f32[112,2432]{1,0:T(8,128)S(1)}, u32[]{:S(2)}) copy-start(f32[112,2432]{1,0:T(8,128)S(1)} %get-tuple-element.419) | copy-start | bytes 3268612
  329.3 15.8 %copy-start.3 = (f32[112,2432]{1,0:T(8,128)}, f32[112,2432]{1,0:T(8,128)S(1)}, u32[]{:S(2)}) copy-start(f32[112,2432]{1,0:T(8,128)S(1)} %get-tuple-element.435) | copy-start | bytes 3268612
  344.1 1.1 copy-start.5
Sparse Core Ops, SparseCore 0:
  9.9 40.0 all-gather.9
  51.9 37.3 all-gather.7
  250.8 70.1 reduce-scatter.1
  345.3 55.6 all-gather.5
where the time goes:
time: 415 us
  waiting for transfers between devices  323 us (78%)
  matrix products  31.5 us (8%)
  other arithmetic  18.7 us (5%)
  between operations  15.2 us (4%)
  blocking collectives  13.3 us (3%)
  local copies, waits for them, and re-layouts  7.47 us (2%)
  starting transfers between devices  5.46 us (1%)
    ppermute x4, waiting for transfers between devices, shifted(): lax.ppermute(value, axis, [(source, source + steps) for source in range(f...  120 us
    reduce_scatter x1, waiting for transfers between devices, shards(): lax.psum_scatter(lax.dot_general(columns, grads_all, (((0,), (0,)), ((),...  70.1 us
    all_gather x1, waiting for transfers between devices, shards(): lax.all_gather(stacked, 'dp', axis=0, tiled=True)  55.1 us
    all_gather x1, waiting for transfers between devices, shards(): lax.all_gather(quant_up[0], 'dp', axis=0, tiled=True)  39.3 us
    all_gather x1, waiting for transfers between devices, shards(): lax.all_gather(quant_gate[0], 'dp', axis=0, tiled=True)  37.4 us
    pmax x1, blocking collectives, shards(): lax.pmax((jnp.max(jnp.abs(new_gate)), jnp.max(jnp.abs(new_up))), 'dp')  13.3 us
    dot_general x3, matrix products, transposed(): lax.dot_general(first_op, second_op, (((1,), (1,)), ((), ())), preferred_...  9.75 us
  transfers between devices with their start and end apart: 8, of which 8 were waited for; matrix products, arithmetic and copies ran while one was open for 1% of the time, Pallas kernels for 0%

commit v1 on v0

v1 whole, which is shorter than its diff:
```python
import jax
import jax.numpy as jnp
from jax import lax
from jax.sharding import PartitionSpec as P

beta_one = 0.9
beta_two = 0.95
learn_rate = 0.002
decay_rate = 0.1
adam_steps = 100.0
norm_eps = 1e-06
adam_eps = 1e-08
scale_eps = 1e-06


def normalize(inputs, norm_gain):
    widened = inputs.astype(jnp.float32)
    inverse = lax.rsqrt(jnp.mean(widened * widened, axis=-1, keepdims=True) + norm_eps)
    return (widened, inverse, (widened * inverse * norm_gain).astype(jnp.bfloat16))


def transposed(first_op, second_op):
    return lax.dot_general(
        first_op, second_op, (((1,), (1,)), ((), ())), preferred_element_type=jnp.float32
    )


def adam_update(master, moment_old, second_old, gradient):
    moment_one = beta_one * moment_old + (1.0 - beta_one) * gradient
    moment_two = beta_two * second_old + (1.0 - beta_two) * gradient * gradient
    unbiased_one = moment_one / (1.0 - beta_one**adam_steps)
    unbiased_two = moment_two / (1.0 - beta_two**adam_steps)
    updated = master - learn_rate * (
        unbiased_one / (jnp.sqrt(unbiased_two) + adam_eps) + decay_rate * master
    )
    return (updated, moment_one, moment_two)


def ring_max(value, axis):
    count = lax.axis_size(axis)
    span = 1
    while span < count:
        pairs = [(source, (source + span) % count) for source in range(count)]
        value = jnp.maximum(value, lax.ppermute(value, axis, pairs))
        span *= 2
    return value


def shards(
    section_inputs,
    cotangent,
    norm_gain,
    quant_gate,
    quant_up,
    scales,
    down_proj,
    master_gate,
    master_up,
    moment_gate,
    moment_up,
    second_gate,
    second_up,
    next_inputs,
):
    gain_row = norm_gain[0]
    scale_pair = scales[0]
    down_local = down_proj[0]
    hidden_count = quant_gate.shape[2]
    sections = lax.axis_size("section")
    position = lax.axis_index("section")
    is_last = position == sections - 1
    both_full = lax.all_gather(
        jnp.concatenate([quant_gate[0], quant_up[0]], axis=1), "dp", axis=0, tiled=True
    )
    widened, inverse, normed = normalize(section_inputs[0], gain_row)
    both_pre = jnp.dot(normed, both_full, preferred_element_type=jnp.float32)
    gate_pre = both_pre[:, :hidden_count] * scale_pair[0]
    up_pre = both_pre[:, hidden_count:] * scale_pair[1]
    sigmoid = jax.nn.sigmoid(gate_pre)
    up_factor = gate_pre * sigmoid
    gate_factor = up_pre * (sigmoid * (1.0 + gate_pre * (1.0 - sigmoid)))
    cubed = inverse * inverse * inverse

    def stage(upstream):
        hidden_grad = transposed(upstream, down_local)
        gate_grad = (hidden_grad * gate_factor).astype(jnp.bfloat16)
        up_grad = (hidden_grad * up_factor).astype(jnp.bfloat16)
        normed_grad = (
            transposed(gate_grad, both_full[:, :hidden_count]) * scale_pair[0]
            + transposed(up_grad, both_full[:, hidden_count:]) * scale_pair[1]
        )
        gained = gain_row * normed_grad
        mean_term = jnp.mean(widened * gained, axis=-1, keepdims=True)
        result = upstream.astype(jnp.float32) + inverse * gained - widened * cubed * mean_term
        return (result.astype(jnp.bfloat16), gate_grad, up_grad)

    upstream = cotangent
    for turn in range(sections):
        result, gate_grad, up_grad = stage(upstream)
        if turn < sections - 1:
            incoming = lax.ppermute(
                result, "section", [(source, source - 1) for source in range(1, sections)]
            )
            upstream = jnp.where(is_last, cotangent, incoming)

    grads_all = jnp.concatenate([gate_grad, up_grad], axis=1)
    summed = lax.psum_scatter(
        lax.dot_general(
            normed, grads_all, (((0,), (0,)), ((), ())), preferred_element_type=jnp.float32
        ).astype(jnp.bfloat16),
        "dp",
        scatter_dimension=0,
        tiled=True,
    ).astype(jnp.float32)
    new_gate, mom_gate, sec_gate = adam_update(
        master_gate[0], moment_gate[0], second_gate[0], summed[:, :hidden_count]
    )
    new_up, mom_up, sec_up = adam_update(
        master_up[0], moment_up[0], second_up[0], summed[:, hidden_count:]
    )
    peaks = jnp.stack([jnp.max(jnp.abs(new_gate)), jnp.max(jnp.abs(new_up))])
    new_scales = ring_max(peaks, "dp") + scale_eps
    unused_one, unused_two, next_normed = normalize(next_inputs[0], gain_row)
    stacked = jnp.concatenate([new_gate, new_up], axis=1).astype(jnp.bfloat16)
    both_next = jnp.dot(
        next_normed,
        lax.all_gather(stacked, "dp", axis=0, tiled=True),
        preferred_element_type=jnp.float32,
    )
    next_hidden = (
        jax.nn.silu(both_next[:, :hidden_count]) * both_next[:, hidden_count:]
    ).astype(jnp.bfloat16)
    return (
        result[None],
        new_gate[None],
        new_up[None],
        mom_gate[None],
        mom_up[None],
        sec_gate[None],
        sec_up[None],
        new_scales[None, :],
        next_hidden[None],
    )


def solution(mesh):
    placed = (
        P("section", "dp", None),
        P("dp", None),
        P("section", None),
        P("section", "dp", None),
        P("section", "dp", None),
        P("section", None),
        P("section", None, None),
        P("section", "dp", None),
        P("section", "dp", None),
        P("section", "dp", None),
        P("section", "dp", None),
        P("section", "dp", None),
        P("section", "dp", None),
        P("section", "dp", None),
    )
    return jax.shard_map(
        shards,
        mesh=mesh,
        in_specs=placed,
        out_specs=(
            P("section", "dp", None),
            P("section", "dp", None),
            P("section", "dp", None),
            P("section", "dp", None),
            P("section", "dp", None),
            P("section", "dp", None),
            P("section", "dp", None),
            P("section", None),
            P("section", "dp", None),
        ),
        check_vma=False,
    )
```

time: 415 us -> 310 us (0.75)
  waiting for transfers between devices: 323 us -> 199 us
  matrix products: 31.5 us -> 59.8 us
  blocking collectives: 13.3 us -> 0 us
  other arithmetic: 18.7 us -> 27.3 us
  local copies, waits for them, and re-layouts: 7.47 us -> 2.33 us
    ppermute x4 -> x6, waiting for transfers between devices: 120 us -> 47.3 us  [the longest x3 37.4 us: shards(): lax.ppermute(result, 'section', [(source, source - 1) for source in range...]
    dot_general x3 -> x12, matrix products: 9.75 us -> 42.6 us  [transposed(): lax.dot_general(first_op, second_op, (((1,), (1,)), ((), ())), preferred_...]
    all_gather x1, waiting for transfers between devices: 55.1 us -> 26.5 us  [shards(): lax.all_gather(stacked, 'dp', axis=0, tiled=True)]
    all_gather x2 -> x1, waiting for transfers between devices: 76.7 us -> 53.3 us  [shards(): lax.all_gather(jnp.concatenate([quant_gate[0], quant_up[0]], axis=1), 'dp...]
    pmax x1 -> x0, blocking collectives: 13.3 us -> none  [shards(): lax.pmax((jnp.max(jnp.abs(new_gate)), jnp.max(jnp.abs(new_up))), 'dp')]
    another operation x1 -> x2, other arithmetic: 0.01 us -> 7.78 us
    reduce_max x1, other arithmetic: 6.87 us -> 0.77 us  [shards(): peaks = jnp.stack([jnp.max(jnp.abs(new_gate)), jnp.max(jnp.abs(new_up))])]
    dot_general x4 -> x3, matrix products: 21.8 us -> 17.2 us  [the longest x1 5.97 us: shards(): lax.dot_general(normed, grads_all, (((0,), (0,)), ((), ())), preferred_el...]
  transfers between devices with their start and end apart: 8 -> 9, of which waited for: 8 -> 9; matrix products, arithmetic and copies ran while one was open for 1% -> 8% of each run, Pallas kernels for 0% -> 0%
where the time goes in v1:
time: 310 us; the launch traced here: 309 us
  waiting for transfers between devices  199 us (64%)
  matrix products  59.8 us (19%)
  other arithmetic  27.3 us (9%)
  between operations  14.3 us (5%)
  starting transfers between devices  6.44 us (2%)
    reduce_scatter x1, waiting for transfers between devices, shards(): lax.psum_scatter(lax.dot_general(normed, grads_all, (((0,), (0,)), ((), (...  71.9 us
    all_gather x1, waiting for transfers between devices, shards(): lax.all_gather(jnp.concatenate([quant_gate[0], quant_up[0]], axis=1), 'dp...  53.3 us
    dot_general x12, matrix products, transposed(): lax.dot_general(first_op, second_op, (((1,), (1,)), ((), ())), preferred_...  42.6 us
    ppermute x3, waiting for transfers between devices, shards(): lax.ppermute(result, 'section', [(source, source - 1) for source in range...  37.4 us
    all_gather x1, waiting for transfers between devices, shards(): lax.all_gather(stacked, 'dp', axis=0, tiled=True)  26.5 us
    ppermute x3, waiting for transfers between devices, ring_max(): value = jnp.maximum(value, lax.ppermute(value, axis, pairs))  9.93 us
    another operation x1, other arithmetic  6.41 us
  transfers between devices with their start and end apart: 9, of which 9 were waited for; matrix products, arithmetic and copies ran while one was open for 8% of the time, Pallas kernels for 0%

profile of v1, /device:TPU:0, one launch (start us, length us, event | category | flops | bytes accessed | tf_op | source)
XLA Modules:
  0.0 309.2 jit_solution(18054944690767434914)
XLA Ops:
  7.3 2.3 pad_maximum_fusion
  10.5 5.2 %fusion.6 = f32[256,2432]{1,0:T(8,128)} fusion(bf16[256,896]{1,0:T(8,128)(2,1)S(1)} %copy-done.2, bf16[1,2432,896]{2,1,0:T(8,128)(2,1)} %param.20), kind=kOutput, calls=%fused_computation.7 | convolution fusion | flops 1115684864 | bytes 7307264 | tf_op jit(solution)/shard_map/dot_general | solution.py:23
  15.8 53.3 %all-gather.3.cloned.1.call-done = bf16[896,4864]{1,0:T(8,128)(2,1)} async-done(((bf16[112,4864]{1,0:T(8,128)(2,1)}), bf16[896,4864]{1,0:T(8,128)(2,1)}) %all-gather.3.cloned.1.call-update) | async-done | bytes 8716304 | tf_op jit(solution)/shard_map/all_gather | solution.py:72
  69.0 5.7 %fusion.118 = f32[256,4864]{1,0:T(8,128)S(1)} fusion(bf16[896,4864]{1,0:T(8,128)(2,1)} %all-gather.3.cloned.1.call-done, bf16[1,256,896]{2,1,0:T(8,128)(2,1)S(1)} %copy-done.1, f32[896]{0:T(1024)S(1)} %reduce, f32[256]{0:T(256)S(1)} %get-tuple-element.24), kind=kOutput, calls=%fused_computation.121 | convolution fusion | flops 2232287232 | bytes 14160384 | tf_op jit(solution)/shard_map/dot_general | solution.py:76
  74.7 4.0 %fusion.25 = f32[256,2432]{1,0:T(8,128)S(1)} fusion(f32[256,4864]{1,0:T(8,128)S(1)} %fusion.118, f32[]{:T(128)} %bitcast.6, f32[]{:T(128)} %bitcast.5), kind=kLoop, calls=%fused_computation.29 | loop fusion | flops 6225920 | bytes 7471112 | tf_op jit(solution)/shard_map/mul | solution.py:81
  78.7 2.8 fusion.70
  81.5 2.4 fusion.103
  86.3 13.6 %collective-permute-done = bf16[256,896]{1,0:T(8,128)(2,1)} collective-permute-done((bf16[256,896]{1,0:T(8,128)(2,1)}, bf16[256,896]{1,0:T(8,128)(2,1)}, u32[]{:S(2)}, u32[]{:S(2)}) %collective-permute-start) | collective-permute-done | bytes 458784 | tf_op jit(solution)/shard_map/ppermute | solution.py:101
  99.9 4.1 %fusion.4 = f32[256,2432]{1,0:T(8,128)S(1)} fusion(bf16[1,2432,896]{2,1,0:T(8,128)(2,1)} %param.20, bf16[256,896]{1,0:T(8,128)(2,1)S(1)} %copy-done.2, bf16[256,896]{1,0:T(8,128)(2,1)} %collective-permute-done, pred[]{:T(512)S(6)} %eq.3), kind=kOutput, calls=%fused_computation.5 | convolution fusion | flops 1115914240 | bytes 7766017 | tf_op jit(solution)/shard_map/dot_general | solution.py:23
  104.0 6.3 %fusion.73 = f32[256,896]{1,0:T(8,128)S(1)} fusion(bf16[896,4864]{1,0:T(8,128)(2,1)} %all-gather.3.cloned.1.call-done, f32[256,2432]{1,0:T(8,128)S(1)} %fusion.4, f32[]{:T(128)} %bitcast.5, f32[256,4864]{1,0:T(8,128)} %copy-done.3, f32[]{:T(128)} %bitcast.6), kind=kOutput, calls=%fused_computation.69 | convolution fusion | flops 1120272384 | bytes 10257408 | tf_op jit(solution)/shard_map/dot_general | solution.py:23
  110.4 2.5 fusion.104
  112.9 1.5 fusion.95
  114.4 1.6 collective-permute-start.1
  116.0 12.3 %collective-permute-done.1 = bf16[256,896]{1,0:T(8,128)(2,1)S(1)} collective-permute-done((bf16[256,896]{1,0:T(8,128)(2,1)S(1)}, bf16[256,896]{1,0:T(8,128)(2,1)S(1)}, u32[]{:S(2)}, u32[]{:S(2)}) %collective-permute-start.1) | collective-permute-done | bytes 458784 | tf_op jit(solution)/shard_map/ppermute | solution.py:101
  128.3 1.6 fusion.2
  129.9 2.8 fusion.76
  132.8 2.5 fusion.105
  136.9 11.5 %collective-permute-done.2 = bf16[256,896]{1,0:T(8,128)(2,1)S(1)} collective-permute-done((bf16[256,896]{1,0:T(8,128)(2,1)S(1)}, bf16[256,896]{1,0:T(8,128)(2,1)S(1)}, u32[]{:S(2)}, u32[]{:S(2)}) %collective-permute-start.2) | collective-permute-done | bytes 458784 | tf_op jit(solution)/shard_map/ppermute | solution.py:101
  148.4 2.5 multiply_convert_fusion.1
  152.4 6.0 %convolution_convert_fusion = bf16[896,4864]{1,0:T(8,128)(2,1)} fusion(bf16[256,2432]{1,0:T(8,128)(2,1)S(1)} %get-tuple-element.18, bf16[256,2432]{1,0:T(8,128)(2,1)S(1)} %get-tuple-element.17, bf16[1,256,896]{2,1,0:T(8,128)(2,1)S(1)} %copy-done.1, f32[896]{0:T(1024)S(1)} %reduce, f32[256]{0:T(256)S(1)} %get-tuple-element.24), kind=kOutput, calls=%fused_computation | convolution fusion | flops 2241626112 | bytes 11670016 | tf_op jit(solution)/shard_map/dot_general | solution.py:108
  158.6 71.9 %reduce-scatter.2.cloned.1.call-done = bf16[112,4864]{1,0:T(8,128)(2,1)} async-done(((bf16[896,4864]{1,0:T(8,128)(2,1)}), bf16[112,4864]{1,0:T(8,128)(2,1)}) %reduce-scatter.2.cloned.1.call-update) | async-done | bytes 1089552 | tf_op jit(solution)/shard_map/reduce_scatter | solution.py:107
  230.5 1.4 convert_element_type.96
  231.9 6.4 %fusion.124 = (bf16[112,2432]{1,0:T(8,128)(2,1)S(1)}, f32[112,2432]{1,0:T(8,128)S(1)}, f32[1,112,2432]{2,1,0:T(8,128)}, f32[1,112,2432]{2,1,0:T(8,128)}, f32[1,1...) fusion(f32[1,112,2432]{2,1,0:T(8,128)} %param.25, ...), kind=kLoop, calls=%fused_computation.132 | loop fusion | flops 8716288 | bytes 16343040 | tf_op jit(solution)/shard_map/convert.2
  240.4 4.8 %fusion.79 = f32[256,896]{1,0:T(8,128)S(1)} fusion(bf16[256,2432]{1,0:T(8,128)(2,1)} %copy-done.12, bf16[896,4864]{1,0:T(8,128)(2,1)} %all-gather.3.cloned.1.call-done, f32[]{:T(128)} %bitcast.5), kind=kOutput, calls=%fused_computation.71 | convolution fusion | flops 1115914240 | bytes 6521344 | tf_op jit(solution)/shard_map/dot_general | solution.py:23
  245.3 5.1 %fusion.106 = (f32[256]{0:T(256)S(1)}, f32[256,896]{1,0:T(8,128)S(1)}) fusion(bf16[1,256,896]{2,1,0:T(8,128)(2,1)S(1)} %copy-done.1, f32[256,896]{1,0:T(8,128)S(1)} %fusion.79, f32[]{:T(128)} %bitcast.6, bf16[256,2432]{1,0:T(8,128)(2,1)S(1)} %copy-done.11, bf16[896,4864]{1,0:T(8,128)(2,1)} %all-gather.3.cloned.1.call-done, f32[896]{0:T(1024)S(1)} %copy-done.9), kind=kOutput, calls=%fused_computation.108 | convolution fusion | flops 1117060864 | bytes 7902208 | tf_op jit(solution)/shard_map/dot_general | solution.py:23
  253.7 3.9 %collective-permute-done.3 = f32[2]{0:T(128)S(1)} collective-permute-done((f32[2]{0:T(128)S(1)}, f32[2]{0:T(128)S(1)}, u32[]{:S(2)}, u32[]{:S(2)}) %collective-permute-start.3) | collective-permute-done | bytes 40 | tf_op jit(solution)/shard_map/ppermute | solution.py:44
  259.5 3.9 %collective-permute-done.4 = f32[2]{0:T(128)S(1)} collective-permute-done((f32[2]{0:T(128)S(1)}, f32[2]{0:T(128)S(1)}, u32[]{:S(2)}, u32[]{:S(2)}) %collective-permute-start.4) | collective-permute-done | bytes 40 | tf_op jit(solution)/shard_map/ppermute | solution.py:44
  264.8 1.4 collective-permute-start.5
  266.2 2.1 collective-permute-done.5
  268.8 26.5 %all-gather.5.cloned.1.call-done = bf16[896,4864]{1,0:T(8,128)(2,1)} async-done(((bf16[112,4864]{1,0:T(8,128)(2,1)}), bf16[896,4864]{1,0:T(8,128)(2,1)}) %all-gather.5.cloned.1.call-update) | async-done | bytes 8716304 | tf_op jit(solution)/shard_map/all_gather | solution.py:127
  295.4 5.5 %fusion.108 = f32[256,4864]{1,0:T(8,128)S(1)} fusion(bf16[896,4864]{1,0:T(8,128)(2,1)} %all-gather.5.cloned.1.call-done, bf16[1,256,896]{2,1,0:T(8,128)(2,1)S(1)} %copy-done.7, f32[256]{0:T(256)} %add_rsqrt_fusion, f32[896]{0:T(1024)} %copy-done.8), kind=kOutput, calls=%fused_computation.110 | convolution fusion | flops 2232287232 | bytes 14160384 | tf_op jit(solution)/shard_map/dot_general | solution.py:125
  300.9 1.7 fusion.82
  (88 shorter events, 15.8 us)
Async XLA Ops:
  7.2 2.5 copy-start.20
  7.2 3.1 %copy-start.1 = (bf16[1,256,896]{2,1,0:T(8,128)(2,1)S(1)}, bf16[1,256,896]{2,1,0:T(8,128)(2,1)}, u32[]{:S(2)}) copy-start(bf16[1,256,896]{2,1,0:T(8,128)(2,1)} %param.14) | copy-start | bytes 1376260
  7.2 3.3 %copy-start.2 = (bf16[256,896]{1,0:T(8,128)(2,1)S(1)}, bf16[256,896]{1,0:T(8,128)(2,1)}, u32[]{:S(2)}) copy-start(bf16[256,896]{1,0:T(8,128)(2,1)} %param.15) | copy-start | bytes 1376260
  7.2 61.8 %all-gather.3.cloned.1.call-start = ((), (), s32[]{:S(2)}) async-start(), calls=%async_computation.1 | async-start | bytes 9805824 | tf_op jit(solution)/shard_map/all_gather | solution.py:72
  9.6 220.9 %reduce-scatter.2.cloned.1.call-start = ((), (), s32[]{:S(2)}) async-start(), calls=%async_computation.2 | async-start | bytes 9805824 | tf_op jit(solution)/shard_map/reduce_scatter | solution.py:107
  9.7 141.2 %copy-start.8 = (f32[896]{0:T(1024)}, f32[896]{0:T(1024)S(1)}, u32[]{:S(2)}) copy-start(f32[896]{0:T(1024)S(1)} %reduce) | copy-start | bytes 10756
  10.5 124.7 %copy-start.17 = (f32[256]{0:T(256)}, f32[256]{0:T(256)S(1)}, u32[]{:S(2)}) copy-start(f32[256]{0:T(256)S(1)} %get-tuple-element.23) | copy-start | bytes 3076
  10.5 140.4 %copy-start.15 = (f32[256]{0:T(256)}, f32[256]{0:T(256)S(1)}, u32[]{:S(2)}) copy-start(f32[256]{0:T(256)S(1)} %get-tuple-element.24) | copy-start | bytes 3076
  69.0 9.7 %copy-start = (bf16[896,4864]{1,0:T(8,128)(2,1)S(1)}, bf16[896,4864]{1,0:T(8,128)(2,1)}, u32[]{:S(2)}) copy-start(bf16[896,4864]{1,0:T(8,128)(2,1)} %all-gather.3.cloned.1.call-done) | copy-start | bytes 26148868
  74.7 4.0 %copy-start.3 = (f32[256,4864]{1,0:T(8,128)}, f32[256,4864]{1,0:T(8,128)S(1)}, u32[]{:S(2)}) copy-start(f32[256,4864]{1,0:T(8,128)S(1)} %fusion.118) | copy-start | bytes 14942212
  74.7 4.0 %copy-start.4 = (f32[256,2432]{1,0:T(8,128)S(1)}, f32[256,2432]{1,0:T(8,128)}, u32[]{:S(2)}) copy-start(f32[256,2432]{1,0:T(8,128)} %fusion.6) | copy-start | bytes 7471108
  85.0 14.9 %collective-permute-start = (bf16[256,896]{1,0:T(8,128)(2,1)}, bf16[256,896]{1,0:T(8,128)(2,1)}, u32[]{:S(2)}, u32[]{:S(2)}) collective-permute-start(bf16[256,896]{1,0:T(8,128)(2,1)} %fusion.93), channel_id=1, source_target_pairs={{8,0},{16,8},{24,16},{9,1},{17,9},{25,17},{10,2},{18,10},{26,18},{... | collective-permute-start | bytes 1376264 | tf_op jit(solution)/shard_map/ppermute | solution.py:101
  99.9 10.4 %slice-start = ((s8[8716288]{0:T(1024)(128)(4,1)}), s8[4194304]{0:T(1024)(128)(4,1)S(1)}, s32[]{:S(2)}) async-start(s8[8716288]{0:T(1024)(128)(4,1)} %bitcast.107), calls=%async_computation.4 | async-start | bytes 8388608
  99.9 28.4 %slice-start.3 = ((s8[4358144]{0:T(1024)(128)(4,1)}), s8[4194304]{0:T(1024)(128)(4,1)S(1)}, s32[]{:S(2)}) async-start(s8[4358144]{0:T(1024)(128)(4,1)} %bitcast.109), calls=%async_computation.7 | async-start | bytes 8388608
  104.0 6.3 %slice-start.1 = ((s8[8716288]{0:T(1024)(128)(4,1)}), s8[4194304]{0:T(1024)(128)(4,1)S(1)}, s32[]{:S(2)}) async-start(s8[8716288]{0:T(1024)(128)(4,1)} %bitcast.107), calls=%async_computation.5 | async-start | bytes 8388608
  104.0 6.3 %slice-start.2 = ((s8[8716288]{0:T(1024)(128)(4,1)}), s8[327680]{0:T(1024)(128)(4,1)S(1)}, s32[]{:S(2)}) async-start(s8[8716288]{0:T(1024)(128)(4,1)} %bitcast.107), calls=%async_computation.6 | async-start | bytes 655360
  104.0 24.3 %slice-start.4 = ((s8[4358144]{0:T(1024)(128)(4,1)}), s8[163840]{0:T(1024)(128)(4,1)S(1)}, s32[]{:S(2)}) async-start(s8[4358144]{0:T(1024)(128)(4,1)} %bitcast.109), calls=%async_computation.8 | async-start | bytes 327680
  112.8 17.0 %slice-start.5 = ((s8[4980736]{0:T(1024)(128)(4,1)}), s8[4194304]{0:T(1024)(128)(4,1)S(1)}, s32[]{:S(2)}) async-start(s8[4980736]{0:T(1024)(128)(4,1)} %bitcast.111), calls=%async_computation.9 | async-start | bytes 8388608
  114.4 15.5 %slice-start.6 = ((s8[4980736]{0:T(1024)(128)(4,1)}), s8[786432]{0:T(1024)(128)(4,1)S(1)}, s32[]{:S(2)}) async-start(s8[4980736]{0:T(1024)(128)(4,1)} %bitcast.111), calls=%async_computation.10 | async-start | bytes 1572864
  114.4 13.9 %collective-permute-start.1 = (bf16[256,896]{1,0:T(8,128)(2,1)S(1)}, bf16[256,896]{1,0:T(8,128)(2,1)S(1)}, u32[]{:S(2)}, u32[]{:S(2)}) collective-permute-start(bf16[256,896]{1,0:T(8,128)(2,1)S(1)} %fusion.95), channel_id=1, source_target_pairs={{8,0},{16,8},{24,16},{9,1},{17,9},{25,17},{10,2},{18,10},{26,18},{... | collective-permute-start | bytes 1376264 | tf_op jit(solution)/shard_map/ppermute | solution.py:101
  135.6 12.8 %collective-permute-start.2 = (bf16[256,896]{1,0:T(8,128)(2,1)S(1)}, bf16[256,896]{1,0:T(8,128)(2,1)S(1)}, u32[]{:S(2)}, u32[]{:S(2)}) collective-permute-start(bf16[256,896]{1,0:T(8,128)(2,1)S(1)} %fusion.97), channel_id=1, source_target_pairs={{8,0},{16,8},{24,16},{9,1},{17,9},{25,17},{10,2},{18,10},{26,18},{... | collective-permute-start | bytes 1376264 | tf_op jit(solution)/shard_map/ppermute | solution.py:101
  158.4 137.0 %all-gather.5.cloned.1.call-start = ((), (), s32[]{:S(2)}) async-start(), calls=%async_computation.3 | async-start | bytes 9805824 | tf_op jit(solution)/shard_map/all_gather | solution.py:127
  238.3 13.3 %copy-start.5 = (f32[112,2432]{1,0:T(8,128)}, f32[112,2432]{1,0:T(8,128)S(1)}, u32[]{:S(2)}) copy-start(f32[112,2432]{1,0:T(8,128)S(1)} %get-tuple-element.10) | copy-start | bytes 3268612
  238.3 13.3 %copy-start.6 = (f32[112,2432]{1,0:T(8,128)}, f32[112,2432]{1,0:T(8,128)S(1)}, u32[]{:S(2)}) copy-start(f32[112,2432]{1,0:T(8,128)S(1)} %get-tuple-element.22) | copy-start | bytes 3268612
  240.4 4.8 %copy-start.9 = (f32[896]{0:T(1024)S(1)}, f32[896]{0:T(1024)}, u32[]{:S(2)}) copy-start(f32[896]{0:T(1024)} %copy-done.8) | copy-start | bytes 10756
  240.4 4.8 %copy-start.11 = (bf16[256,2432]{1,0:T(8,128)(2,1)S(1)}, bf16[256,2432]{1,0:T(8,128)(2,1)}, u32[]{:S(2)}) copy-start(bf16[256,2432]{1,0:T(8,128)(2,1)} %copy-done.10) | copy-start | bytes 3735556
  245.3 5.2 %copy-start.14 = (bf16[256,896]{1,0:T(8,128)(2,1)S(1)}, bf16[256,896]{1,0:T(8,128)(2,1)}, u32[]{:S(2)}) copy-start(bf16[256,896]{1,0:T(8,128)(2,1)} %copy-done.13) | copy-start | bytes 1376260
  245.3 5.2 %copy-start.16 = (f32[256]{0:T(256)S(1)}, f32[256]{0:T(256)}, u32[]{:S(2)}) copy-start(f32[256]{0:T(256)} %copy-done.15) | copy-start | bytes 3076
  245.3 5.2 %copy-start.18 = (f32[256]{0:T(256)S(1)}, f32[256]{0:T(256)}, u32[]{:S(2)}) copy-start(f32[256]{0:T(256)} %copy-done.17) | copy-start | bytes 3076
  253.7 3.9 %collective-permute-start.3 = (f32[2]{0:T(128)S(1)}, f32[2]{0:T(128)S(1)}, u32[]{:S(2)}, u32[]{:S(2)}) collective-permute-start(f32[2]{0:T(128)S(1)} %pad_maximum_fusion.2), channel_id=1, source_target_pairs={{0,1},{1,2},{2,3},{3,4},{4,5},{5,6},{6,7},{7,0},{8,9},{9,10},{10,1... | collective-permute-start | bytes 32 | tf_op jit(solution)/shard_map/ppermute | solution.py:44
  259.0 4.4 %collective-permute-start.4 = (f32[2]{0:T(128)S(1)}, f32[2]{0:T(128)S(1)}, u32[]{:S(2)}, u32[]{:S(2)}) collective-permute-start(f32[2]{0:T(128)S(1)} %fusion.132), channel_id=1, source_target_pairs={{0,2},{1,3},{2,4},{3,5},{4,6},{5,7},{6,0},{7,1},{8,10},{9,11},{10,... | collective-permute-start | bytes 32 | tf_op jit(solution)/shard_map/ppermute | solution.py:44
  264.8 3.5 %collective-permute-start.5 = (f32[2]{0:T(128)S(1)}, f32[2]{0:T(128)S(1)}, u32[]{:S(2)}, u32[]{:S(2)}) collective-permute-start(f32[2]{0:T(128)S(1)} %fusion.133), channel_id=1, source_target_pairs={{0,4},{1,5},{2,6},{3,7},{4,0},{5,1},{6,2},{7,3},{8,12},{9,13},{10,... | collective-permute-start | bytes 32 | tf_op jit(solution)/shard_map/ppermute | solution.py:44
  (5 other events, 8.8 us)
Sparse Core Ops, SparseCore 0:
  10.5 58.4 all-gather.2
  158.5 72.0 reduce-scatter.1
  239.6 55.7 all-gather.4
